TPU v7x, 128 devices: a whole 4x4x4 slice. The times are simulated.
128 devices in a mesh: segment: 2 (over core), fsdp: 32 (over x, y_lo, z), dp: 2 (over y_hi).
Axes of the slice: x: 4, y: 4 (y_hi: 2, y_lo: 2; y = y_hi * 2 + y_lo), z: 4, core: 2. Of those that a mesh axis runs over, the one named last changes fastest.
Arguments:
- hooks: bfloat16 [2, 4, 256, 64, 6144], P('segment', 'dp', 'fsdp'), may hold values from -6 to 6
- proj_weight: bfloat16 [2, 6144, 256], P('segment', 'fsdp'), may hold values from -0.078125 to 0.078125
- conv_weight: bfloat16 [2, 2, 2304, 256], P('segment', None, 'fsdp'), may hold values from -0.125 to 0.125
- head_weight: bfloat16 [3, 256], replicated, may hold values from -0.375 to 0.375
- light_color: float32 [25, 3], replicated, may hold values from 0.3 to 1.5
- illum: int32 [4, 4], P('dp'), may hold values from 0 to 24
- offsets: int32 [4, 4, 2], P('dp'), may hold values from 0 to 32
- photos: bfloat16 [4, 4, 3, 96, 96], P('dp'), may hold values from 0 to 10
Outputs:
- grad_proj: float32 [2, 6144, 256], P('segment', 'fsdp')
- grad_conv: float32 [2, 2, 2304, 256], P('segment', None, 'fsdp')
- grad_head: float32 [3, 256], replicated
- loss: float32 [], replicated
All inputs are finite; a program needn't handle non-finite values.
Results may differ from a plain program's by a relative error of at most 0.018.
Values may be sent and summed in bfloat16 or wider, within the bound.
A program may use at most 128 MiB of HBM per device.

v0:
```python
import jax
import jax.numpy as jnp
from jax import lax
from jax.sharding import PartitionSpec as P

LOSS_SCALE = 8192.0


def extended(shard, sides, width):
    for axis, dim in sides:
        size, length = (lax.axis_size(axis), shard.shape[dim])
        up = [(i, (i + 1) % size) for i in range(size - 1)]
        down = [(j, i) for i, j in up]
        last = lax.slice_in_dim(shard, length - width, length, axis=dim)
        initial = lax.slice_in_dim(shard, 0, width, axis=dim)
        before = lax.ppermute(last, axis, up)
        after = lax.ppermute(initial, axis, down)
        shard = jnp.concatenate([before, shard, after], axis=dim)
    return shard


def shifted(shard, axis, by):
    size = lax.axis_size(axis)
    pairs = [(i, i + by) for i in range(size) if 0 <= i + by < size]
    return lax.ppermute(shard, axis, pairs)


def activate(values):
    return jax.nn.gelu(values, approximate=True)


def activate_slope(values):
    return jax.vjp(activate, values)[1](jnp.ones_like(values))[0]


def patches(field):
    rows_here, cols_here, channels = (field.shape[1], field.shape[2], field.shape[3])
    padded = extended(field, (("fsdp", 1),), 1)
    row_base = lax.axis_index("fsdp") * rows_here % cols_here
    upper = jnp.where(row_base == 0, jnp.zeros_like(padded[:, :1]), padded[:, :1])
    lower = jnp.where(
        row_base + rows_here == cols_here, jnp.zeros_like(padded[:, -1:]), padded[:, -1:]
    )
    padded = jnp.concatenate([upper, padded[:, 1:-1], lower], axis=1)
    padded = jnp.pad(padded, ((0, 0), (0, 0), (1, 1), (0, 0)))
    pieces = [
        padded[:, i : i + rows_here, j : j + cols_here, :] for i in range(3) for j in range(3)
    ]
    return jnp.concatenate(pieces, axis=-1).reshape(-1, 9 * channels)


def contract_rows(left, right):
    return lax.dot_general(
        left, right, (((0,), (0,)), ((), ())), preferred_element_type=jnp.float32
    )


def flipped(kernel):
    channels = kernel.shape[1]
    grid_form = kernel.reshape(3, 3, channels, channels)[::-1, ::-1]
    return jnp.swapaxes(grid_form, 2, 3).reshape(9 * channels, channels)


def section_parts(segment_in, first_conv, second_conv):
    channels = segment_in.shape[-1]
    first_in = activate(segment_in.astype(jnp.float32)).astype(jnp.bfloat16)
    first_patches = patches(first_in)
    hidden = jnp.dot(first_patches, first_conv, preferred_element_type=jnp.float32)
    second_in = activate(hidden).astype(jnp.bfloat16).reshape(segment_in.shape)
    second_patches = patches(second_in)
    update = jnp.dot(second_patches, second_conv, preferred_element_type=jnp.float32)
    output = (segment_in.reshape(-1, channels).astype(jnp.float32) + update).astype(jnp.bfloat16)
    return (output.reshape(segment_in.shape), first_patches, hidden, second_patches)


def section_back(segment_in, out_grad, first_conv, second_conv, first_flip, second_flip):
    channels = segment_in.shape[-1]
    output, first_patches, hidden, second_patches = section_parts(
        segment_in, first_conv, second_conv
    )
    out_rows = out_grad.reshape(-1, channels)
    second_grad = jnp.dot(patches(out_grad), second_flip, preferred_element_type=jnp.float32)
    hidden_grad = (second_grad * activate_slope(hidden)).astype(jnp.bfloat16)
    first_grad = jnp.dot(
        patches(hidden_grad.reshape(segment_in.shape)),
        first_flip,
        preferred_element_type=jnp.float32,
    )
    slope = activate_slope(segment_in.reshape(-1, channels).astype(jnp.float32))
    in_grad = (
        (out_rows.astype(jnp.float32) + first_grad * slope)
        .astype(jnp.bfloat16)
        .reshape(segment_in.shape)
    )
    return (
        in_grad,
        contract_rows(first_patches, hidden_grad),
        contract_rows(second_patches, out_rows),
    )


def head_loss(output, head_weight, tints, targets, factor):
    channels = output.shape[-1]
    out_rows = output.reshape(-1, channels)
    logits = lax.dot_general(
        head_weight, out_rows, (((1,), (1,)), ((), ())), preferred_element_type=jnp.float32
    )
    albedo = jax.nn.sigmoid(logits.reshape(targets.shape))
    tint = jnp.transpose(tints)[:, :, None, None]
    mismatch = albedo * tint - targets
    squares = jnp.sum(mismatch * mismatch)
    logit_grad = (
        (factor * mismatch * tint * albedo * (1.0 - albedo)).astype(jnp.bfloat16).reshape(3, -1)
    )
    head_grad = lax.dot_general(
        logit_grad, out_rows, (((1,), (0,)), ((), ())), preferred_element_type=jnp.float32
    )
    out_grad = lax.dot_general(
        logit_grad, head_weight, (((0,), (0,)), ((), ())), preferred_element_type=jnp.float32
    )
    return (squares, head_grad, out_grad.astype(jnp.bfloat16).reshape(output.shape))


def crop_tints(illum, light_color):
    lights = light_color.shape[0]
    onehot = (illum[..., None] == jnp.arange(lights, dtype=jnp.int32)).astype(jnp.float32)
    return jnp.dot(onehot.reshape(-1, lights), light_color, precision=lax.Precision.HIGHEST)


def crop_targets(photos, offsets, row_base, rows_here, cols_here):

    def one_crop(picture, offset):
        start = (jnp.zeros((), jnp.int32), offset[0] + row_base, offset[1])
        return lax.dynamic_slice(picture, start, (3, rows_here, cols_here))

    cut = jax.vmap(jax.vmap(one_crop))(photos, offsets).astype(jnp.float32)
    return jnp.moveaxis(cut, 2, 0)


def fetch_convs(conv_weight):
    gathered = lax.all_gather(conv_weight[0], "fsdp", axis=1, tiled=True)
    return (gathered[0], gathered[1])


def pass_on(field):
    return shifted(field, "segment", 1)


def pass_back(field):
    return shifted(field, "segment", -1)


def body(hooks, proj_weight, conv_weight, head_weight, light_color, illum, offsets, photos):
    segments = lax.axis_size("segment")
    segment_index = lax.axis_index("segment")
    is_last = segment_index == segments - 1
    micro_count, band_rows, grid_cols, model_width = (
        hooks.shape[1],
        hooks.shape[2],
        hooks.shape[3],
        hooks.shape[4],
    )
    crop_count = 1
    channels = proj_weight.shape[2]
    tokens = hooks[0].reshape(-1, model_width)
    first_global = lax.axis_index("fsdp") * band_rows
    crop_here = first_global // grid_cols
    row_base = first_global % grid_cols
    columns = tokens
    projected = jnp.dot(
        columns,
        lax.all_gather(proj_weight[0], "fsdp", axis=0, tiled=True),
        preferred_element_type=jnp.float32,
    )
    projected = projected.astype(jnp.bfloat16).reshape(
        micro_count, crop_count, band_rows, grid_cols, channels
    )
    first_conv, second_conv = fetch_convs(conv_weight)
    micro_shape = (crop_count, band_rows, grid_cols, channels)
    flat_shape = (micro_count * crop_count, band_rows, grid_cols, channels)
    flat_proj = projected.reshape(flat_shape)
    incoming = jnp.zeros_like(flat_proj)
    for p in range(segments):
        segment_in = (flat_proj.astype(jnp.float32) + incoming.astype(jnp.float32)).astype(
            jnp.bfloat16
        )
        output = section_parts(segment_in, first_conv, second_conv)[0]
        if p + 1 < segments:
            incoming = pass_on(output)
    inputs_all = segment_in.reshape((micro_count,) + micro_shape)
    outputs_all = output.reshape((micro_count,) + micro_shape)
    illum_here = lax.dynamic_slice_in_dim(illum, crop_here, 1, 1)
    offsets_here = lax.dynamic_slice_in_dim(offsets, crop_here, 1, 1)
    photos_here = lax.dynamic_slice_in_dim(photos, crop_here, 1, 1)
    tints = crop_tints(illum_here, light_color)
    targets = crop_targets(photos_here, offsets_here, row_base, band_rows, grid_cols)
    targets = targets.reshape(3, micro_count * crop_count, band_rows, grid_cols)
    npix = 3 * micro_count * lax.axis_size("dp") * band_rows * lax.axis_size("fsdp") * grid_cols
    factor = 2.0 * LOSS_SCALE / npix
    squares, head_grad, out_grads = head_loss(
        outputs_all.reshape(flat_shape), head_weight, tints, targets, factor
    )
    out_grads = out_grads.reshape((micro_count,) + micro_shape)
    back_first, back_second = fetch_convs(conv_weight)
    first_flip = flipped(back_first)
    second_flip = flipped(back_second)
    flat_in = inputs_all.reshape(flat_shape)
    flat_grads = out_grads.reshape(flat_shape)
    received = jnp.zeros_like(flat_grads)
    for p in range(segments):
        out_grad = jnp.where(is_last, flat_grads, received)
        in_grad, first_sum, second_sum = section_back(
            flat_in, out_grad, back_first, back_second, first_flip, second_flip
        )
        if p + 1 < segments:
            received = pass_back(in_grad)
    grad_rows = in_grad.reshape(-1, channels)
    conv_sums = jnp.concatenate([first_sum, second_sum], axis=1)
    columns = tokens
    proj_part = lax.psum_scatter(
        contract_rows(columns, grad_rows), "fsdp", scatter_dimension=0, tiled=True
    )
    conv_part = lax.psum_scatter(conv_sums, "fsdp", scatter_dimension=0, tiled=True)
    proj_part, conv_part = lax.psum((proj_part, conv_part), "dp")
    loss_term = jnp.where(is_last, squares, 0.0)
    head_term = jnp.where(is_last, head_grad, 0.0)
    head_total, square_total = lax.psum((head_term, loss_term), ("segment", "fsdp", "dp"))
    grad_conv = jnp.stack([conv_part[:, :channels], conv_part[:, channels:]])[None]
    return (proj_part[None], grad_conv, head_total, square_total / npix)


def solution(mesh):
    placed = (
        P("segment", "dp", "fsdp", None, None),
        P("segment", "fsdp", None),
        P("segment", None, "fsdp", None),
        P(),
        P(),
        P("dp", None),
        P("dp", None, None),
        P("dp", None, None, None, None),
    )
    return jax.shard_map(
        body,
        mesh=mesh,
        in_specs=placed,
        out_specs=(P("segment", "fsdp", None), P("segment", None, "fsdp", None), P(), P()),
        check_vma=False,
    )
```

profile of v0, /device:TPU:1, one launch (start us, length us, event | category | flops | bytes accessed | tf_op | source)
XLA Modules:
  0.0 882.3 jit_solution(2431889212769604529)
XLA Ops:
  9.6 138.4 %all-gather.5.cloned.1.call-done = bf16[1,6144,256]{2,1,0:T(8,128)(2,1)} async-done(((bf16[1,192,256]{2,1,0:T(8,128)(2,1)}), bf16[1,6144,256]{2,1,0:T(8,128)(2,1)}) %all-gather.5.cloned.1.call-update) | async-done | bytes 3145744 | tf_op jit(solution)/shard_map/all_gather | solution.py:172
  147.9 7.3 fusion.8
  157.1 4.0 collective-permute-start
  171.4 132.0 %all-gather.7.cloned.1.call-done = bf16[1,2,2304,256]{3,2,1,0:T(8,128)(2,1)} async-done(((bf16[1,2,72,256]{3,2,1,0:T(8,128)(2,1)}), bf16[1,2,2304,256]{3,2,1,0:T(8,128)(2,1)}) %all-gather.7.cloned.1.call-update) | async-done | bytes 2359312 | tf_op jit(solution)/shard_map/all_gather | solution.py:141
  303.4 4.2 fusion.54
  307.6 3.0 collective-permute-start.2
  312.0 4.4 collective-permute-done.3
  319.0 1.4 fusion.11
  321.9 12.9 %copy.50 = bf16[2,1,3,96,96]{2,1,0,4,3:T(2,128)(2,1)} copy(bf16[2,1,3,96,96]{4,3,2,1,0:T(8,128)(2,1)S(1)} %constant_dynamic-slice_fusion.2) | data formatting | bytes 221184
  334.8 3.3 gather_fusion
  339.5 5.5 collective-permute-done.4
  345.4 1.6 collective-permute-start.5
  347.1 1.8 fusion.92
  348.9 1.8 collective-permute-start.6
  350.7 3.2 collective-permute-done.6
  355.9 2.5 multiply_convert_fusion
  358.4 1.9 collective-permute-start.7
  361.7 3.6 collective-permute-done.8
  367.5 1.8 copy-done.12
  369.2 1.4 fusion.12
  373.5 1.6 copy.40
  375.8 4.1 collective-permute-start.9
  383.4 1.8 fusion.13
  385.2 3.6 collective-permute-start.11
  389.5 1.5 collective-permute-start.12
  391.0 3.7 collective-permute-done.12
  396.0 1.4 fusion.4
  397.4 23.5 %collective-permute-start.13 = (bf16[2,8,64,256]{3,2,1,0:T(8,128)(2,1)S(1)}, bf16[2,8,64,256]{3,2,1,0:T(8,128)(2,1)S(1)}, u32[]{:S(2)}, u32[]{:S(2)}) collective-permute-start(bf16[2,8,64,256]{3,2,1,0:T(8,128)(2,1)S(1)} %bitcast.225), channel_id=1, source_target_pairs={{64,0},{65,1},{66,2},{67,3},{68,4},{69,5},{70,6},{71,7},{72,8},{73... | collective-permute-start | bytes 1572872 | tf_op jit(solution)/shard_map/ppermute | solution.py:25
  420.9 1.5 collective-permute-done.13
  422.4 4.8 collective-permute-start.14
  428.6 1.5 convolution_bitcast_fusion.1
  430.1 4.8 collective-permute-done.15
  436.1 1.8 fusion.14
  438.2 1.5 fusion.104
  439.7 2.5 pad_maximum_fusion
  442.2 6.1 copy.48
  448.4 5.8 collective-permute-start.16
  454.1 1.5 collective-permute-start.17
  455.7 3.5 collective-permute-done.17
  460.5 2.2 copy-done.11
  462.7 16.0 %convolution_bitcast_fusion = f32[6144,256]{0,1:T(8,128)} fusion(bf16[1024,6144]{1,0:T(8,128)(2,1)} %bitcast.223, bf16[1024,256]{1,0:T(8,128)(2,1)S(1)} %bitcast.150, f32[1024,256]{1,0:T(8,128)S(1)} %fusion.36, bf16[1024,2304]{1,0:T(8,128)(2,1)} %copy-done.11, bf16[2304,256]{1,0:T(8,128)(2,1)S(1)} %bitcast.207), kind=kOutput, calls=%fused_computation.1 | convolution fusion | flops 4430233600 | bytes 26345472 | tf_op jit(solution)/shard_map/dot_general | solution.py:53
  478.7 6.6 copy.46
  485.7 119.6 %reduce-scatter.9.cloned.1.call-done = f32[72,512]{1,0:T(8,128)} async-done(((f32[2304,512]{1,0:T(8,128)}), f32[72,512]{1,0:T(8,128)}) %reduce-scatter.9.cloned.1.call-update) | async-done | bytes 147472
  605.3 1.7 copy.49
  607.1 171.1 %reduce-scatter.7.cloned.1.call-done = f32[192,256]{1,0:T(8,128)} async-done(((f32[6144,256]{1,0:T(8,128)}), f32[192,256]{1,0:T(8,128)}) %reduce-scatter.7.cloned.1.call-update) | async-done | bytes 196624
  778.2 1.8 copy.47
  782.0 88.2 %all-reduce.8 = (f32[3,256]{1,0:T(4,128)}, f32[]{:T(128)}) all-reduce(f32[3,256]{1,0:T(4,128)S(1)} %convolution_select_fusion, f32[]{:T(128)S(6)} %select_n.191), channel_id=1, replica_groups=mesh['segment'=2,'fsdp'=32,'dp'=2] {'segment','fsdp','dp'}, use_global_device_ids=true, to_apply=%region_4.5 | all-reduce | flops 769 | bytes 6152 | tf_op jit(solution)/shard_map/psum | solution.py:227
  872.7 1.7 copy.43
  (224 shorter events, 43.6 us)
Async XLA Ops:
  7.2 303.4 %copy-start = (bf16[2,4,3,96,96]{4,3,2,1,0:T(8,128)(2,1)S(1)}, bf16[2,4,3,96,96]{4,3,2,1,0:T(8,128)(2,1)}, u32[]{:S(2)}) copy-start(bf16[2,4,3,96,96]{4,3,2,1,0:T(8,128)(2,1)} %param.15) | copy-start | bytes 1327108
  7.2 140.8 %all-gather.5.cloned.1.call-start = ((), (), s32[]{:S(2)}) async-start(), calls=%async_computation.2 | async-start | bytes 3244032 | tf_op jit(solution)/shard_map/all_gather | solution.py:172
  7.9 295.4 %all-gather.7.cloned.1.call-start = ((), (), s32[]{:S(2)}) async-start(), calls=%async_computation.3 | async-start | bytes 2433024 | tf_op jit(solution)/shard_map/all_gather | solution.py:141
  8.7 596.7 %reduce-scatter.9.cloned.1.call-start = ((), (), s32[]{:S(2)}) async-start(), calls=%async_computation.5 | async-start | bytes 4866048
  155.6 5.4 collective-permute-start.1
  157.1 5.3 collective-permute-start
  307.6 4.4 collective-permute-start.2
  310.6 5.7 collective-permute-start.3
  317.3 1.7 copy-start.4
  320.4 24.6 %collective-permute-start.4 = (bf16[2,8,64,256]{3,2,1,0:T(8,128)(2,1)S(1)}, bf16[2,8,64,256]{3,2,1,0:T(8,128)(2,1)S(1)}, u32[]{:S(2)}, u32[]{:S(2)}) collective-permute-start(bf16[2,8,64,256]{3,2,1,0:T(8,128)(2,1)S(1)} %bitcast.224), channel_id=1, source_target_pairs={{0,64},{1,65},{2,66},{3,67},{4,68},{5,69},{6,70},{7,71},{8,72},{9,... | collective-permute-start | bytes 1572872 | tf_op jit(solution)/shard_map/ppermute | solution.py:25
  321.9 16.8 %copy-start.15 = (s32[2,4]{1,0:T(2,128)S(1)}, s32[2,4]{1,0:T(2,128)}, u32[]{:S(2)}) copy-start(s32[2,4]{1,0:T(2,128)} %param.13) | copy-start | bytes 100
  321.9 16.9 %copy-start.16 = (f32[25,3]{0,1:T(4,128)S(1)}, f32[25,3]{0,1:T(4,128)}, u32[]{:S(2)}) copy-start(f32[25,3]{0,1:T(4,128)} %param.12) | copy-start | bytes 904
  338.1 10.7 %copy-start.9 = (bf16[2,3,8,64]{1,0,3,2:T(2,128)(2,1)}, bf16[2,3,8,64]{1,0,3,2:T(2,128)(2,1)S(1)}, u32[]{:S(2)}) copy-start(bf16[2,3,8,64]{1,0,3,2:T(2,128)(2,1)S(1)} %gather_fusion) | copy-start | bytes 18436
  345.4 23.8 %copy-start.2 = (f32[2,8,64,256]{3,2,1,0:T(8,128)}, f32[2,8,64,256]{3,2,1,0:T(8,128)S(1)}, u32[]{:S(2)}) copy-start(f32[2,8,64,256]{3,2,1,0:T(8,128)S(1)} %get-tuple-element.29) | copy-start | bytes 3145732
  345.4 5.2 collective-permute-start.5
  348.9 5.0 collective-permute-start.6
  354.3 1.7 copy-start.5
  355.1 3.3 copy-start.13
  358.4 3.3 collective-permute-start.7
  360.3 5.0 collective-permute-start.8
  367.1 2.2 copy-start.12
  369.2 1.4 copy-start.14
  370.6 0.8 copy-start.6
  372.1 7.7 collective-permute-start.10
  375.8 5.7 collective-permute-start.9
  381.8 1.3 copy-start.8
  381.8 1.6 copy-start.17
  383.4 5.4 copy-start.3
  385.2 5.7 collective-permute-start.11
  389.5 5.2 collective-permute-start.12
  396.0 32.6 %slice-start = ((s8[4718592]{0:T(1024)(128)(4,1)}), s8[524288]{0:T(1024)(128)(4,1)S(1)}, s32[]{:S(2)}) async-start(s8[4718592]{0:T(1024)(128)(4,1)} %bitcast.211), calls=%async_computation.7 | async-start | bytes 1048576
  396.0 32.6 %slice-start.1 = ((s8[4718592]{0:T(1024)(128)(4,1)}), s8[4194304]{0:T(1024)(128)(4,1)S(1)}, s32[]{:S(2)}) async-start(s8[4718592]{0:T(1024)(128)(4,1)} %bitcast.211), calls=%async_computation.8 | async-start | bytes 8388608
  397.4 25.0 %collective-permute-start.13 = (bf16[2,8,64,256]{3,2,1,0:T(8,128)(2,1)S(1)}, bf16[2,8,64,256]{3,2,1,0:T(8,128)(2,1)S(1)}, u32[]{:S(2)}, u32[]{:S(2)}) collective-permute-start(bf16[2,8,64,256]{3,2,1,0:T(8,128)(2,1)S(1)} %bitcast.225), channel_id=1, source_target_pairs={{64,0},{65,1},{66,2},{67,3},{68,4},{69,5},{70,6},{71,7},{72,8},{73... | collective-permute-start | bytes 1572872 | tf_op jit(solution)/shard_map/ppermute | solution.py:25
  422.4 7.7 collective-permute-start.14
  427.3 7.6 collective-permute-start.15
  435.9 2.2 slice-start.2
  436.1 2.1 slice-start.3
  448.3 329.9 %reduce-scatter.7.cloned.1.call-start = ((), (), s32[]{:S(2)}) async-start(), calls=%async_computation.4 | async-start | bytes 6488064
  448.4 7.3 collective-permute-start.16
  454.1 5.0 collective-permute-start.17
  460.5 2.2 copy-start.11
  485.3 294.7 %copy-start.10 = (bf16[2,3,8,64]{1,0,3,2:T(2,128)(2,1)S(1)}, bf16[2,3,8,64]{1,0,3,2:T(2,128)(2,1)}, u32[]{:S(2)}) copy-start(bf16[2,3,8,64]{1,0,3,2:T(2,128)(2,1)} %copy-done.9) | copy-start | bytes 18436
  485.3 296.5 %copy-start.7 = (bf16[1024,256]{1,0:T(8,128)(2,1)S(1)}, bf16[1024,256]{1,0:T(8,128)(2,1)}, u32[]{:S(2)}) copy-start(bf16[1024,256]{1,0:T(8,128)(2,1)} %copy-done.6) | copy-start | bytes 1572868
  485.3 389.2 %copy-start.1 = (bf16[2,4,3,96,96]{4,3,2,1,0:T(8,128)(2,1)S(1)}, bf16[2,4,3,96,96]{4,3,2,1,0:T(8,128)(2,1)}, u32[]{:S(2)}) copy-start(bf16[2,4,3,96,96]{4,3,2,1,0:T(8,128)(2,1)} %param.15) | copy-start | bytes 1327108
  485.3 385.6 %all-reduce.12.cloned.1.call-start = ((), (), s32[]{:S(2)}) async-start(), calls=%async_computation.6 | async-start | bytes 1048576 | tf_op jit(solution)/shard_map/psum | solution.py:224
Sparse Core Ops, SparseCore 0:
  9.7 138.2 all-gather.4
  149.6 153.7 all-gather.6
  448.4 156.8 reduce-scatter.8
  607.6 170.5 reduce-scatter.6
  780.5 55.5 all-reduce.11
where the time goes:
time: 890 us; the launch traced here: 882 us
  waiting for transfers between devices  595 us (67%)
  blocking collectives  88.2 us (10%)
  starting transfers between devices  65 us (7%)
  local copies, waits for them, and re-layouts  62.2 us (7%)
  matrix products  41.6 us (5%)
  between operations  17.8 us (2%)
  other arithmetic  12.8 us (1%)
    unnamed x7, waiting for transfers between devices  292 us
    all_gather x1, waiting for transfers between devices, body(): lax.all_gather(proj_weight[0], 'fsdp', axis=0, tiled=True)  138 us
    all_gather x1, waiting for transfers between devices, fetch_convs(): gathered = lax.all_gather(conv_weight[0], 'fsdp', axis=1, tiled=True)  132 us
    psum x1, blocking collectives, body(): lax.psum((head_term, loss_term), ('segment', 'fsdp', 'dp'))  88.2 us
    unnamed x114, local copies, waits for them, and re-layouts  46.8 us
    ppermute x8, starting transfers between devices, extended(): before = lax.ppermute(last, axis, up)  28.8 us
    ppermute x2, starting transfers between devices, shifted(): return lax.ppermute(shard, axis, pairs)  24.7 us
    ppermute x8, waiting for transfers between devices, extended(): after = lax.ppermute(initial, axis, down)  23.1 us
  transfers between devices with their start and end apart: 23, of which 14 were waited for; matrix products, arithmetic and copies ran while one was open for 8% of the time, Pallas kernels for 0%

commit v1 on v0

--- a/solution.py
+++ b/solution.py
@@ -169,7 +169,10 @@
     columns = tokens
     projected = jnp.dot(
         columns,
-        lax.all_gather(proj_weight[0], "fsdp", axis=0, tiled=True),
+        jnp.concatenate(
+            lax.all_to_all(jnp.stack([proj_weight[0]] * lax.axis_size("fsdp")), "fsdp", 0, 0),
+            axis=0,
+        ),
         preferred_element_type=jnp.float32,
     )
     projected = projected.astype(jnp.bfloat16).reshape(

time: 890 us -> 759 us (0.85)
  waiting for transfers between devices: 595 us -> 450 us
  starting transfers between devices: 65 us -> 74.8 us
    all_gather x1 -> x0, waiting for transfers between devices: 138 us -> none  [body(): lax.all_gather(proj_weight[0], 'fsdp', axis=0, tiled=True)]
    all_gather x1, waiting for transfers between devices: 132 us -> 90.9 us  [fetch_convs(): gathered = lax.all_gather(conv_weight[0], 'fsdp', axis=1, tiled=True)]
    all_to_all x0 -> x1, waiting for transfers between devices: none -> 39.8 us  [body(): lax.all_to_all(jnp.stack([proj_weight[0]] * lax.axis_size('fsdp')), 'fsdp...]
    all_to_all x0 -> x1, starting transfers between devices: none -> 9.84 us  [body(): lax.all_to_all(jnp.stack([proj_weight[0]] * lax.axis_size('fsdp')), 'fsdp...]
    unnamed x7 -> x6, waiting for transfers between devices: 292 us -> 290 us
    unnamed x114 -> x116, local copies, waits for them, and re-layouts: 46.8 us -> 46.8 us
  transfers between devices with their start and end apart: 23 -> 23, of which waited for: 14 -> 15; matrix products, arithmetic and copies ran while one was open for 8% -> 9% of each run, Pallas kernels for 0% -> 0%
where the time goes in v1:
time: 759 us; the launch traced here: 751 us
  waiting for transfers between devices  450 us (59%)
  blocking collectives  88.9 us (12%)
  starting transfers between devices  74.8 us (10%)
  local copies, waits for them, and re-layouts  64.5 us (8%)
  matrix products  41.6 us (5%)
  between operations  17.9 us (2%)
  other arithmetic  12.8 us (2%)
    unnamed x6, waiting for transfers between devices  290 us
    all_gather x1, waiting for transfers between devices, fetch_convs(): gathered = lax.all_gather(conv_weight[0], 'fsdp', axis=1, tiled=True)  90.9 us
    psum x1, blocking collectives, body(): lax.psum((head_term, loss_term), ('segment', 'fsdp', 'dp'))  88.9 us
    unnamed x116, local copies, waits for them, and re-layouts  46.8 us
    all_to_all x1, waiting for transfers between devices, body(): lax.all_to_all(jnp.stack([proj_weight[0]] * lax.axis_size('fsdp')), 'fsdp...  39.8 us
    ppermute x8, starting transfers between devices, extended(): before = lax.ppermute(last, axis, up)  29.3 us
    ppermute x2, starting transfers between devices, shifted(): return lax.ppermute(shard, axis, pairs)  24.3 us
    ppermute x8, waiting for transfers between devices, extended(): after = lax.ppermute(initial, axis, down)  23.2 us
  transfers between devices with their start and end apart: 23, of which 15 were waited for; matrix products, arithmetic and copies ran while one was open for 9% of the time, Pallas kernels for 0%

profile of v1, /device:TPU:1, one launch (start us, length us, event | category | flops | bytes accessed | tf_op | source)
XLA Modules:
  0.0 750.7 jit_solution(4492311187762936036)
XLA Ops:
  7.2 3.0 stack.12
  10.2 9.8 %all-to-all-start = ((bf16[32,192,256]{2,1,0:T(8,128)(2,1)}), bf16[32,192,256]{2,1,0:T(8,128)(2,1)}, u32[]{:S(2)}, u32[]{:S(2)}) async-start(bf16[32,192,256]{2,1,0:T(8,128)(2,1)} %stack.12), calls=%async_computation | async-start | bytes 6291456 | tf_op jit(solution)/shard_map/all_to_all | solution.py:173
  20.9 39.8 %all-to-all-done = bf16[32,192,256]{2,1,0:T(8,128)(2,1)} async-done(((bf16[32,192,256]{2,1,0:T(8,128)(2,1)}), bf16[32,192,256]{2,1,0:T(8,128)(2,1)}, u32[]{:S(2)}, u32[]{:S(2)}) %all-to-all-start) | async-done | bytes 3145760 | tf_op jit(solution)/shard_map/all_to_all | solution.py:173
  60.7 7.3 fusion.7
  69.9 4.0 collective-permute-start
  84.2 90.9 %all-gather.3.cloned.1.call-done = bf16[1,2,2304,256]{3,2,1,0:T(8,128)(2,1)} async-done(((bf16[1,2,72,256]{3,2,1,0:T(8,128)(2,1)}), bf16[1,2,2304,256]{3,2,1,0:T(8,128)(2,1)}) %all-gather.3.cloned.1.call-update) | async-done | bytes 2359312 | tf_op jit(solution)/shard_map/all_gather | solution.py:141
  175.1 4.2 fusion.47
  179.3 2.7 collective-permute-start.2
  183.4 4.1 collective-permute-done.3
  193.0 12.9 %copy.50 = bf16[2,1,3,96,96]{2,1,0,4,3:T(2,128)(2,1)} copy(bf16[2,1,3,96,96]{4,3,2,1,0:T(8,128)(2,1)S(1)} %constant_dynamic-slice_fusion.2) | data formatting | bytes 221184
  205.9 3.3 gather_fusion
  210.7 3.4 collective-permute-done.4
  214.5 1.6 collective-permute-start.5
  216.1 1.8 fusion.85
  217.9 1.8 collective-permute-start.6
  219.7 3.2 collective-permute-done.6
  224.9 2.5 multiply_convert_fusion
  227.4 1.9 collective-permute-start.7
  230.8 3.6 collective-permute-done.8
  236.5 1.8 copy-done.12
  242.5 1.6 copy.40
  244.8 4.5 collective-permute-start.9
  252.8 1.8 fusion.5
  254.6 3.6 collective-permute-start.11
  258.9 1.5 collective-permute-start.12
  260.4 3.7 collective-permute-done.12
  265.5 1.4 fusion.2
  266.9 23.0 %collective-permute-start.13 = (bf16[2,8,64,256]{3,2,1,0:T(8,128)(2,1)S(1)}, bf16[2,8,64,256]{3,2,1,0:T(8,128)(2,1)S(1)}, u32[]{:S(2)}, u32[]{:S(2)}) collective-permute-start(bf16[2,8,64,256]{3,2,1,0:T(8,128)(2,1)S(1)} %bitcast.222), channel_id=1, source_target_pairs={{64,0},{65,1},{66,2},{67,3},{68,4},{69,5},{70,6},{71,7},{72,8},{73... | collective-permute-start | bytes 1572872 | tf_op jit(solution)/shard_map/ppermute | solution.py:25
  289.9 1.5 collective-permute-done.13
  291.5 5.2 collective-permute-start.14
  298.1 1.5 convolution_bitcast_fusion.1
  299.6 4.8 collective-permute-done.15
  305.6 1.8 fusion.6
  307.7 1.5 fusion.97
  309.2 2.5 pad_maximum_fusion
  311.6 6.1 copy.48
  317.8 5.8 collective-permute-start.16
  323.6 1.5 collective-permute-start.17
  325.1 3.5 collective-permute-done.17
  330.0 2.2 copy-done.11
  332.1 16.0 %convolution_bitcast_fusion = f32[6144,256]{0,1:T(8,128)} fusion(bf16[1024,6144]{1,0:T(8,128)(2,1)} %bitcast.220, bf16[1024,256]{1,0:T(8,128)(2,1)S(1)} %bitcast.146, f32[1024,256]{1,0:T(8,128)S(1)} %fusion.29, bf16[1024,2304]{1,0:T(8,128)(2,1)} %copy-done.11, bf16[2304,256]{1,0:T(8,128)(2,1)S(1)} %bitcast.203), kind=kOutput, calls=%fused_computation.1 | convolution fusion | flops 4430233600 | bytes 26345472 | tf_op jit(solution)/shard_map/dot_general | solution.py:53
  348.1 6.6 copy.46
  355.2 118.0 %reduce-scatter.9.cloned.1.call-done = f32[72,512]{1,0:T(8,128)} async-done(((f32[2304,512]{1,0:T(8,128)}), f32[72,512]{1,0:T(8,128)}) %reduce-scatter.9.cloned.1.call-update) | async-done | bytes 147472
  473.1 1.7 copy.49
  474.9 171.0 %reduce-scatter.7.cloned.1.call-done = f32[192,256]{1,0:T(8,128)} async-done(((f32[6144,256]{1,0:T(8,128)}), f32[192,256]{1,0:T(8,128)}) %reduce-scatter.7.cloned.1.call-update) | async-done | bytes 196624
  645.9 1.8 copy.47
  649.7 88.9 %all-reduce.8 = (f32[3,256]{1,0:T(4,128)}, f32[]{:T(128)}) all-reduce(f32[3,256]{1,0:T(4,128)S(1)} %convolution_select_fusion, f32[]{:T(128)S(6)} %select_n.191), channel_id=1, replica_groups=mesh['segment'=2,'fsdp'=32,'dp'=2] {'segment','fsdp','dp'}, use_global_device_ids=true, to_apply=%region_4.5 | all-reduce | flops 769 | bytes 6152 | tf_op jit(solution)/shard_map/psum | solution.py:230
  741.1 1.7 copy.43
  (226 shorter events, 44.9 us)
Async XLA Ops:
  7.2 174.9 %copy-start = (bf16[2,4,3,96,96]{4,3,2,1,0:T(8,128)(2,1)S(1)}, bf16[2,4,3,96,96]{4,3,2,1,0:T(8,128)(2,1)}, u32[]{:S(2)}) copy-start(bf16[2,4,3,96,96]{4,3,2,1,0:T(8,128)(2,1)} %param.15) | copy-start | bytes 1327108
  7.2 13.7 %copy-start.15 = (s32[2,4,2]{1,2,0:T(2,128)S(1)}, s32[2,4,2]{1,2,0:T(2,128)}, u32[]{:S(2)}) copy-start(s32[2,4,2]{1,2,0:T(2,128)} %param.14) | copy-start | bytes 196
  10.2 50.5 %all-to-all-start = ((bf16[32,192,256]{2,1,0:T(8,128)(2,1)}), bf16[32,192,256]{2,1,0:T(8,128)(2,1)}, u32[]{:S(2)}, u32[]{:S(2)}) async-start(bf16[32,192,256]{2,1,0:T(8,128)(2,1)} %stack.12), calls=%async_computation | async-start | bytes 6291456 | tf_op jit(solution)/shard_map/all_to_all | solution.py:173
  20.0 155.1 %all-gather.3.cloned.1.call-start = ((), (), s32[]{:S(2)}) async-start(), calls=%async_computation.3 | async-start | bytes 2433024 | tf_op jit(solution)/shard_map/all_gather | solution.py:141
  20.8 452.4 %reduce-scatter.9.cloned.1.call-start = ((), (), s32[]{:S(2)}) async-start(), calls=%async_computation.5 | async-start | bytes 4866048
  68.4 5.8 collective-permute-start.1
  69.9 5.4 collective-permute-start
  179.3 4.0 collective-permute-start.2
  182.1 5.4 collective-permute-start.3
  188.4 1.7 copy-start.4
  191.5 22.5 %collective-permute-start.4 = (bf16[2,8,64,256]{3,2,1,0:T(8,128)(2,1)S(1)}, bf16[2,8,64,256]{3,2,1,0:T(8,128)(2,1)S(1)}, u32[]{:S(2)}, u32[]{:S(2)}) collective-permute-start(bf16[2,8,64,256]{3,2,1,0:T(8,128)(2,1)S(1)} %bitcast.221), channel_id=1, source_target_pairs={{0,64},{1,65},{2,66},{3,67},{4,68},{5,69},{6,70},{7,71},{8,72},{9,... | collective-permute-start | bytes 1572872 | tf_op jit(solution)/shard_map/ppermute | solution.py:25
  193.0 16.8 %copy-start.16 = (s32[2,4]{1,0:T(2,128)S(1)}, s32[2,4]{1,0:T(2,128)}, u32[]{:S(2)}) copy-start(s32[2,4]{1,0:T(2,128)} %param.13) | copy-start | bytes 100
  193.0 16.9 %copy-start.17 = (f32[25,3]{0,1:T(4,128)S(1)}, f32[25,3]{0,1:T(4,128)}, u32[]{:S(2)}) copy-start(f32[25,3]{0,1:T(4,128)} %param.12) | copy-start | bytes 904
  209.2 8.7 %copy-start.9 = (bf16[2,3,8,64]{1,0,3,2:T(2,128)(2,1)}, bf16[2,3,8,64]{1,0,3,2:T(2,128)(2,1)S(1)}, u32[]{:S(2)}) copy-start(bf16[2,3,8,64]{1,0,3,2:T(2,128)(2,1)S(1)} %gather_fusion) | copy-start | bytes 18436
  214.4 23.8 %copy-start.2 = (f32[2,8,64,256]{3,2,1,0:T(8,128)}, f32[2,8,64,256]{3,2,1,0:T(8,128)S(1)}, u32[]{:S(2)}) copy-start(f32[2,8,64,256]{3,2,1,0:T(8,128)S(1)} %get-tuple-element.29) | copy-start | bytes 3145732
  214.5 5.2 collective-permute-start.5
  217.9 5.0 collective-permute-start.6
  223.3 1.7 copy-start.5
  224.1 3.3 copy-start.13
  227.4 3.3 collective-permute-start.7
  229.4 5.0 collective-permute-start.8
  236.1 2.2 copy-start.12
  238.2 1.4 copy-start.14
  239.7 0.8 copy-start.6
  241.1 8.1 %collective-permute-start.10 = (bf16[2,1,64,256]{3,2,1,0:T(8,128)(2,1)S(1)}, bf16[2,1,64,256]{3,2,1,0:T(8,128)(2,1)}, u32[]{:S(2)}, u32[]{:S(2)}) collective-permute-start(bf16[2,1,64,256]{3,2,1,0:T(8,128)(2,1)S(1)} %get-tuple-element.68), channel_id=1, source_target_pairs={{2,0},{4,2},{6,4},{8,6},{10,8},{12,10},{14,12},{16,14},{18,16},{20... | collective-permute-start | bytes 196616 | tf_op jit(solution)/shard_map/ppermute | solution.py:17
  244.8 6.1 collective-permute-start.9
  251.2 1.3 copy-start.8
  251.2 1.6 copy-start.18
  252.8 5.4 copy-start.3
  254.6 5.7 collective-permute-start.11
  258.9 5.2 collective-permute-start.12
  265.4 32.6 %slice-start = ((s8[4718592]{0:T(1024)(128)(4,1)}), s8[524288]{0:T(1024)(128)(4,1)S(1)}, s32[]{:S(2)}) async-start(s8[4718592]{0:T(1024)(128)(4,1)} %bitcast.208), calls=%async_computation.7 | async-start | bytes 1048576
  265.4 32.6 %slice-start.1 = ((s8[4718592]{0:T(1024)(128)(4,1)}), s8[4194304]{0:T(1024)(128)(4,1)S(1)}, s32[]{:S(2)}) async-start(s8[4718592]{0:T(1024)(128)(4,1)} %bitcast.208), calls=%async_computation.8 | async-start | bytes 8388608
  266.9 24.5 %collective-permute-start.13 = (bf16[2,8,64,256]{3,2,1,0:T(8,128)(2,1)S(1)}, bf16[2,8,64,256]{3,2,1,0:T(8,128)(2,1)S(1)}, u32[]{:S(2)}, u32[]{:S(2)}) collective-permute-start(bf16[2,8,64,256]{3,2,1,0:T(8,128)(2,1)S(1)} %bitcast.222), channel_id=1, source_target_pairs={{64,0},{65,1},{66,2},{67,3},{68,4},{69,5},{70,6},{71,7},{72,8},{73... | collective-permute-start | bytes 1572872 | tf_op jit(solution)/shard_map/ppermute | solution.py:25
  291.5 8.1 %collective-permute-start.14 = (bf16[2,1,64,256]{3,2,1,0:T(8,128)(2,1)S(1)}, bf16[2,1,64,256]{3,2,1,0:T(8,128)(2,1)S(1)}, u32[]{:S(2)}, u32[]{:S(2)}) collective-permute-start(bf16[2,1,64,256]{3,2,1,0:T(8,128)(2,1)S(1)} %get-tuple-element.61), channel_id=1, source_target_pairs={{0,2},{2,4},{4,6},{6,8},{8,10},{10,12},{12,14},{14,16},{16,18},{18... | collective-permute-start | bytes 196616 | tf_op jit(solution)/shard_map/ppermute | solution.py:16
  296.7 7.6 %collective-permute-start.15 = (bf16[2,1,64,256]{3,2,1,0:T(8,128)(2,1)S(1)}, bf16[2,1,64,256]{3,2,1,0:T(8,128)(2,1)S(1)}, u32[]{:S(2)}, u32[]{:S(2)}) collective-permute-start(bf16[2,1,64,256]{3,2,1,0:T(8,128)(2,1)S(1)} %get-tuple-element.62), channel_id=1, source_target_pairs={{2,0},{4,2},{6,4},{8,6},{10,8},{12,10},{14,12},{16,14},{18,16},{20... | collective-permute-start | bytes 196616 | tf_op jit(solution)/shard_map/ppermute | solution.py:17
  305.3 2.2 slice-start.2
  305.6 2.1 slice-start.3
  317.7 328.2 %reduce-scatter.7.cloned.1.call-start = ((), (), s32[]{:S(2)}) async-start(), calls=%async_computation.4 | async-start | bytes 6488064
  317.8 7.3 collective-permute-start.16
  323.6 5.0 collective-permute-start.17
  330.0 2.2 copy-start.11
  354.7 293.0 %copy-start.10 = (bf16[2,3,8,64]{1,0,3,2:T(2,128)(2,1)S(1)}, bf16[2,3,8,64]{1,0,3,2:T(2,128)(2,1)}, u32[]{:S(2)}) copy-start(bf16[2,3,8,64]{1,0,3,2:T(2,128)(2,1)} %copy-done.9) | copy-start | bytes 18436
  354.7 294.8 %copy-start.7 = (bf16[1024,256]{1,0:T(8,128)(2,1)S(1)}, bf16[1024,256]{1,0:T(8,128)(2,1)}, u32[]{:S(2)}) copy-start(bf16[1024,256]{1,0:T(8,128)(2,1)} %copy-done.6) | copy-start | bytes 1572868
  354.7 388.1 %copy-start.1 = (bf16[2,4,3,96,96]{4,3,2,1,0:T(8,128)(2,1)S(1)}, bf16[2,4,3,96,96]{4,3,2,1,0:T(8,128)(2,1)}, u32[]{:S(2)}) copy-start(bf16[2,4,3,96,96]{4,3,2,1,0:T(8,128)(2,1)} %param.15) | copy-start | bytes 1327108
  354.7 384.5 %all-reduce.12.cloned.1.call-start = ((), (), s32[]{:S(2)}) async-start(), calls=%async_computation.6 | async-start | bytes 1048576 | tf_op jit(solution)/shard_map/psum | solution.py:227
Sparse Core Ops, SparseCore 0:
  22.5 152.5 all-gather.2
  317.9 155.2 reduce-scatter.8
  475.5 170.3 reduce-scatter.6
  648.2 56.5 all-reduce.11
